TPU v7x, 32 devices: a whole 2x2x4 slice. The times are simulated.
32 devices in a mesh: row: 8 (over y, x, core), col: 4 (over z).
Axes of the slice: x: 2, y: 2, z: 4, core: 2. Of those that a mesh axis runs over, the one named last changes fastest.
Arguments:
- hamiltonian: float32 [512, 512], P('row', 'col'), as said below
- tile_mask: int32 [2, 2], replicated, may hold values from 0 to 1, as said below
- start_block: float32 [512, 32], P(('row', 'col')), may hold values from -6 to 6
Outputs:
- states: float32 [512, 32], P(('row', 'col'))
- ritz_matrix: float32 [32, 32], replicated
Inputs may be any that keep to these rules, and one draw needn't show every extreme that they name: tile_mask is symmetric with ones on its diagonal; the share of nonzero tiles differs from tile row to tile row. `hamiltonian`: H is symmetric and H + I is positive definite.
All inputs are finite; a program needn't handle non-finite values.
Results may differ from a plain program's by a relative error of at most 0.0003.
Values sent between devices are 32-bit elements; how exact they have to be, the bound alone decides.
A program may use at most 64 MiB of HBM per device.

v0:
```python
import jax
import jax.numpy as jnp
from jax import lax
from jax.sharding import PartitionSpec as P

TILE = 256
ITERS = 3


HIGH = lax.Precision.HIGHEST


def small_dot(left, right):
    return jnp.dot(left, right, precision=HIGH)


def inner(left, right):
    return lax.dot_general(left, right, (((0,), (0,)), ((), ())), precision=HIGH)


def cho_apply(lower, right):
    first = lax.linalg.triangular_solve(lower, right, left_side=True, lower=True)
    return lax.linalg.triangular_solve(lower, first, left_side=True, lower=True, transpose_a=True)


def gram_sum(first, second):
    return lax.psum((first, second), ("row", "col"))


def ritz_step(basis, basis_image, gram, proj_raw, width):
    proj = 0.5 * (proj_raw + proj_raw.T)
    shifted = proj + 2.0 * gram
    solved = cho_apply(jnp.linalg.cholesky(shifted), gram[:, :width])
    normal_form = small_dot(solved.T, small_dot(gram, solved))
    normal_form = 0.5 * (normal_form + normal_form.T)
    factor = jnp.linalg.cholesky(normal_form)
    coeffs = lax.linalg.triangular_solve(
        factor, solved, left_side=False, lower=True, transpose_a=True
    )
    states = small_dot(basis, coeffs)
    image = small_dot(basis_image, coeffs)
    along = small_dot(basis[:, width:], coeffs[width:])
    along_image = small_dot(basis_image[:, width:], coeffs[width:])
    ritz = small_dot(coeffs.T, small_dot(proj, coeffs))
    return (states, image, along, along_image, ritz)


def body(hamiltonian, tile_mask, start_block):
    row_index = lax.axis_index("row")
    col_index = lax.axis_index("col")
    row_count = lax.axis_size("row")
    col_count = lax.axis_size("col")
    local_rows, local_cols = hamiltonian.shape
    piece = start_block.shape[0]
    width = start_block.shape[1]
    tile_row = (row_index * local_rows + jnp.arange(local_rows)) // TILE
    column = jnp.arange(local_cols)
    vector_index = (column // piece * col_count + col_index) * piece + column % piece
    tile_column = vector_index // TILE
    local_mask = jnp.take(jnp.take(tile_mask, tile_row, axis=0), tile_column, axis=1)
    masked = hamiltonian * local_mask.astype(jnp.float32)

    def operate(vectors):
        gathered = lax.all_gather(vectors, "row", axis=0, tiled=True)
        return lax.psum_scatter(
            jnp.dot(masked, gathered, precision=HIGH), "col", scatter_dimension=0, tiled=True
        )

    states = start_block
    image = operate(states)
    gram, product = gram_sum(inner(states, states), inner(states, image))
    theta = cho_apply(jnp.linalg.cholesky(gram), product)
    resid = image - small_dot(states, theta)
    along = None
    along_image = None
    ritz = theta
    for step in range(ITERS):
        resid_image = operate(resid)
        if along is None:
            basis = jnp.concatenate([states, resid], axis=1)
            basis_image = jnp.concatenate([image, resid_image], axis=1)
        else:
            basis = jnp.concatenate([states, resid, along], axis=1)
            basis_image = jnp.concatenate([image, resid_image, along_image], axis=1)
        gram, proj_raw = gram_sum(inner(basis, basis), inner(basis, basis_image))
        states, image, along, along_image, ritz = ritz_step(
            basis, basis_image, gram, proj_raw, width
        )
        if step + 1 < ITERS:
            resid = image - small_dot(states, ritz)
    total = piece * row_count * col_count
    scale = jnp.sqrt(jnp.float32(total))
    return (states * scale, ritz)


def solution(mesh):
    placed = (P("row", "col"), P(), P(("row", "col"), None))
    return jax.shard_map(
        body, mesh=mesh, in_specs=placed, out_specs=(P(("row", "col"), None), P()), check_vma=False
    )
```

profile of v0, /device:TPU:0, one launch (start us, length us, event | category | flops | bytes accessed | tf_op | source)
XLA Modules:
  0.0 554.9 jit_solution(1504895541638693773)
XLA Ops:
  7.3 0.5 copy-done
  7.8 0.6 gather_fusion
  8.6 0.7 copy-done.9
  9.4 0.6 copy-done.3
  10.0 10.7 %all_gather.12 = f32[128,32]{1,0:T(8,128)S(1)} all-gather(f32[16,32]{1,0:T(8,128)S(1)} %copy-done.3), channel_id=1, replica_groups=mesh['row'=8,'col'=4] {'row'}, dimensions={0}, use_global_device_ids=true | all-gather | bytes 18432 | tf_op jit(solution)/shard_map/all_gather | solution.py:64
  20.7 0.6 gather_fusion.1
  21.4 0.9 fusion.94
  22.5 19.1 %reduce-scatter.5.cloned.1.call-done = f32[16,32]{1,0:T(8,128)} async-done(((f32[64,32]{1,0:T(8,128)}), f32[16,32]{1,0:T(8,128)}) %reduce-scatter.5.cloned.1.call-update) | async-done | bytes 2064 | tf_op jit(solution)/shard_map/reduce_scatter | solution.py:65
  41.7 0.9 convolution_bitcast_fusion.2
  42.6 38.7 %all-reduce.3 = (f32[32,32]{0,1:T(8,128)S(1)}, f32[32,32]{0,1:T(8,128)S(1)}) all-reduce(f32[32,32]{0,1:T(8,128)S(1)} %convolution_bitcast_fusion.2, f32[32,32]{0,1:T(8,128)S(1)} %fusion.95), channel_id=1, replica_groups=mesh['row'=8,'col'=4] {'row','col'}, use_global_device_ids=true, to_apply=%region_4.6 | all-reduce | flops 2048 | bytes 16384 | tf_op jit(solution)/shard_map/psum | solution.py:27
  81.4 2.9 cholesky.151
  84.3 0.6 compare_reduce_fusion.5
  85.0 0.7 fusion.27
  85.6 2.4 custom-call.29
  88.4 0.6 copy-done.6
  89.1 10.0 %all_gather.13 = f32[128,32]{1,0:T(8,128)S(1)} all-gather(f32[16,32]{1,0:T(8,128)S(1)} %fusion), channel_id=1, replica_groups=mesh['row'=8,'col'=4] {'row'}, dimensions={0}, use_global_device_ids=true | all-gather | bytes 18432 | tf_op jit(solution)/shard_map/all_gather | solution.py:64
  99.1 0.9 fusion.96
  100.1 0.3 fusion.93
  100.4 17.7 %reduce-scatter.7.cloned.1.call-done = f32[16,32]{1,0:T(8,128)} async-done(((f32[64,32]{1,0:T(8,128)}), f32[16,32]{1,0:T(8,128)}) %reduce-scatter.7.cloned.1.call-update) | async-done | bytes 2064 | tf_op jit(solution)/shard_map/reduce_scatter | solution.py:65
  118.1 1.0 fusion.71
  119.1 39.0 %all-reduce.2 = (f32[64,64]{1,0:T(8,128)S(1)}, f32[64,64]{0,1:T(8,128)S(1)}) all-reduce(f32[64,64]{1,0:T(8,128)S(1)} %fusion.93, f32[64,64]{0,1:T(8,128)S(1)} %fusion.71), channel_id=1, replica_groups=mesh['row'=8,'col'=4] {'row','col'}, use_global_device_ids=true, to_apply=%region_7.9 | all-reduce | flops 8192 | bytes 65536 | tf_op jit(solution)/shard_map/psum | solution.py:27
  158.3 5.8 %cholesky.57 = f32[64,64]{1,0:T(8,128)S(1)} custom-call(f32[64,64]{1,0:T(8,128)S(1)} %fusion.21), custom_call_target="Cholesky" | custom-call | tf_op jit(solution)/shard_map/jit(cholesky)/cholesky | solution.py:33
  164.2 0.6 compare_reduce_fusion.6
  164.8 0.7 fusion.15
  165.5 4.9 custom-call.30
  171.3 2.9 cholesky.162
  174.3 0.6 compare_reduce_fusion.4
  174.9 0.7 fusion.28
  175.6 2.4 custom-call.31
  179.0 0.6 copy-done.8
  179.9 10.0 %all_gather.14 = f32[128,32]{1,0:T(8,128)S(1)} all-gather(f32[16,32]{1,0:T(8,128)S(1)} %convolution_subtract_fusion.1), channel_id=1, replica_groups=mesh['row'=8,'col'=4] {'row'}, dimensions={0}, use_global_device_ids=true | all-gather | bytes 18432 | tf_op jit(solution)/shard_map/all_gather | solution.py:64
  190.0 0.9 fusion.101
  190.9 0.9 fusion.100
  192.0 17.8 %reduce-scatter.9.cloned.1.call-done = f32[16,32]{1,0:T(8,128)} async-done(((f32[64,32]{1,0:T(8,128)}), f32[16,32]{1,0:T(8,128)}) %reduce-scatter.9.cloned.1.call-update) | async-done | bytes 2064 | tf_op jit(solution)/shard_map/reduce_scatter | solution.py:65
  209.9 1.6 fusion.91
  211.7 123.9 %all-reduce.9.cloned.1.call-done = (f32[96,96]{0,1:T(8,128)}, f32[96,96]{1,0:T(8,128)}) async-done(((f32[96,96]{0,1:T(8,128)}, f32[96,96]{1,0:T(8,128)}), (f32[96,96]{0,1:T(8,128)}, f32[96,96]{1,0:T(8,128)})) %all-reduce.9.cloned.1.call-update) | async-done | bytes 73744 | tf_op jit(solution)/shard_map/psum | solution.py:27
  335.6 0.9 copy.14
  336.7 8.8 %cholesky.173 = f32[96,96]{1,0:T(8,128)S(1)} custom-call(f32[96,96]{1,0:T(8,128)S(1)} %fusion.13), custom_call_target="Cholesky" | custom-call | tf_op jit(solution)/shard_map/jit(cholesky)/cholesky | solution.py:33
  345.5 0.6 compare_reduce_fusion.3
  346.1 0.7 fusion.1
  346.8 7.4 %custom-call.36 = f32[1,96,96]{1,2,0:T(8,128)S(1)} custom-call(f32[1,96,96]{2,1,0:T(8,128)S(1)} %fusion.1), custom_call_target="InvertDiagBlocksLowerTriangular" | custom-call | tf_op jit(solution)/shard_map/triangular_solve/custom-call.9 | solution.py:23
  354.7 0.3 fusion.102
  355.3 2.9 cholesky.184
  358.2 0.6 compare_reduce_fusion.2
  358.9 0.7 fusion.29
  359.5 2.4 custom-call.37
  363.0 0.5 copy-done.7
  363.9 9.2 %all_gather.15 = f32[128,32]{1,0:T(8,128)S(1)} all-gather(f32[16,32]{1,0:T(8,128)S(1)} %convolution_subtract_fusion), channel_id=1, replica_groups=mesh['row'=8,'col'=4] {'row'}, dimensions={0}, use_global_device_ids=true | all-gather | bytes 18432 | tf_op jit(solution)/shard_map/all_gather | solution.py:64
  373.2 0.9 fusion.107
  374.1 0.9 fusion.106
  375.2 19.6 %reduce-scatter.11.cloned.1.call-done = f32[16,32]{1,0:T(8,128)} async-done(((f32[64,32]{1,0:T(8,128)}), f32[16,32]{1,0:T(8,128)}) %reduce-scatter.11.cloned.1.call-update) | async-done | bytes 2064 | tf_op jit(solution)/shard_map/reduce_scatter | solution.py:65
  394.9 1.6 fusion.64
  396.5 123.1 %all-reduce.7.cloned.1.call-done = (f32[96,96]{0,1:T(8,128)}, f32[96,96]{1,0:T(8,128)}) async-done(((f32[96,96]{0,1:T(8,128)}, f32[96,96]{1,0:T(8,128)}), (f32[96,96]{0,1:T(8,128)}, f32[96,96]{1,0:T(8,128)})) %all-reduce.7.cloned.1.call-update) | async-done | bytes 73744 | tf_op jit(solution)/shard_map/psum | solution.py:27
  519.6 0.9 copy.19
  520.7 8.8 %cholesky.195 = f32[96,96]{1,0:T(8,128)S(1)} custom-call(f32[96,96]{1,0:T(8,128)S(1)} %fusion.7), custom_call_target="Cholesky" | custom-call | tf_op jit(solution)/shard_map/jit(cholesky)/cholesky | solution.py:33
  529.5 0.6 compare_reduce_fusion.1
  530.2 0.7 fusion.2
  530.8 7.4 %custom-call.39 = f32[1,96,96]{1,2,0:T(8,128)S(1)} custom-call(f32[1,96,96]{2,1,0:T(8,128)S(1)} %fusion.2), custom_call_target="InvertDiagBlocksLowerTriangular" | custom-call | tf_op jit(solution)/shard_map/triangular_solve/custom-call.9 | solution.py:23
  539.3 2.9 cholesky.206
  542.3 0.6 compare_reduce_fusion
  542.9 0.7 fusion.30
  543.6 2.4 custom-call.40
  546.5 0.7 convolution_multiply_fusion
  547.3 0.8 fusion.110
  (102 shorter events, 8.8 us)
Async XLA Ops:
  7.2 0.7 copy-start
  7.2 34.5 %reduce-scatter.5.cloned.1.call-start = ((), (), s32[]{:S(2)}) async-start(), calls=%async_computation.4 | async-start | bytes 40960 | tf_op jit(solution)/shard_map/reduce_scatter | solution.py:65
  8.5 0.8 copy-start.9
  9.3 0.7 copy-start.3
  22.3 95.8 %reduce-scatter.7.cloned.1.call-start = ((), (), s32[]{:S(2)}) async-start(), calls=%async_computation.5 | async-start | bytes 40960 | tf_op jit(solution)/shard_map/reduce_scatter | solution.py:65
  88.3 0.7 copy-start.6
  100.0 109.8 %reduce-scatter.9.cloned.1.call-start = ((), (), s32[]{:S(2)}) async-start(), calls=%async_computation.6 | async-start | bytes 40960 | tf_op jit(solution)/shard_map/reduce_scatter | solution.py:65
  178.9 0.7 copy-start.8
  191.8 143.8 %all-reduce.9.cloned.1.call-start = ((), (), s32[]{:S(2)}) async-start(), calls=%async_computation.9 | async-start | bytes 196608 | tf_op jit(solution)/shard_map/psum | solution.py:27
  211.5 183.4 %reduce-scatter.11.cloned.1.call-start = ((), (), s32[]{:S(2)}) async-start(), calls=%async_computation.7 | async-start | bytes 40960 | tf_op jit(solution)/shard_map/reduce_scatter | solution.py:65
  335.6 1.0 copy-start.1
  335.6 1.0 copy-start.4
  362.8 0.7 copy-start.7
  375.0 144.6 %all-reduce.7.cloned.1.call-start = ((), (), s32[]{:S(2)}) async-start(), calls=%async_computation.8 | async-start | bytes 196608 | tf_op jit(solution)/shard_map/psum | solution.py:27
  519.6 1.0 copy-start.2
  519.6 1.0 copy-start.5
Sparse Core Ops, SparseCore 0:
  22.4 19.2 reduce-scatter.4
  100.2 17.9 reduce-scatter.6
  191.9 17.9 reduce-scatter.8
  216.3 119.1 all-reduce.8
  375.1 19.7 reduce-scatter.10
  400.4 119.1 all-reduce.6
where the time goes:
time: 556 us; the launch traced here: 555 us
  waiting for transfers between devices  321 us (58%)
  blocking collectives  118 us (21%)
  other arithmetic  74.3 us (13%)
  matrix products  19 us (3%)
  between operations  14.6 us (3%)
  local copies, waits for them, and re-layouts  7.59 us (1%)
    psum x2, waiting for transfers between devices, gram_sum(): return lax.psum((first, second), ('row', 'col'))  247 us
    psum x2, blocking collectives, gram_sum(): return lax.psum((first, second), ('row', 'col'))  77.7 us
    reduce_scatter x4, waiting for transfers between devices, operate(): lax.psum_scatter(jnp.dot(masked, gathered, precision=HIGH), 'col', scatte...  74.3 us
    all_gather x4, blocking collectives, operate(): gathered = lax.all_gather(vectors, 'row', axis=0, tiled=True)  39.9 us
    another operation x9, other arithmetic, ritz_step(): solved = cho_apply(jnp.linalg.cholesky(shifted), gram[:, :width])  25.4 us
    another operation x8, other arithmetic, cho_apply(): lax.linalg.triangular_solve(lower, first, left_side=True, lower=True, tra...  24.7 us
  transfers between devices with their start and end apart: 6, of which 6 were waited for; matrix products, arithmetic and copies ran while one was open for 0% of the time, Pallas kernels for 0%

commit v1 on v0

--- a/solution.py
+++ b/solution.py
@@ -1,13 +1,194 @@
+import functools
+
 import jax
 import jax.numpy as jnp
 from jax import lax
+from jax.experimental import pallas as pl
+from jax.experimental.pallas import tpu as pltpu
 from jax.sharding import PartitionSpec as P
 
 TILE = 256
 ITERS = 3
-
+LANES = 128
+SUB = 8
+LOCAL_BYTES = 4 * 2**20
 
 HIGH = lax.Precision.HIGHEST
+
+
+def dot_nn(left, right):
+    return lax.dot_general(
+        left, right, (((1,), (0,)), ((), ())), precision=HIGH, preferred_element_type=jnp.float32
+    )
+
+
+def dot_nt(left, right):
+    return lax.dot_general(
+        left, right, (((1,), (1,)), ((), ())), precision=HIGH, preferred_element_type=jnp.float32
+    )
+
+
+def lane_splat(tile, lane):
+    return jnp.broadcast_to(tile[:, lane : lane + 1], (SUB, LANES))
+
+
+def row_splat(tile, row):
+    return jnp.broadcast_to(tile[row : row + 1, :], (SUB, LANES))
+
+
+def assemble(rows):
+    sub = lax.broadcasted_iota(jnp.int32, (SUB, LANES), 0)
+    tile = rows[0]
+    for i in range(1, SUB):
+        tile = jnp.where(sub == i, rows[i], tile)
+    return tile
+
+
+def eliminate(tiles, first_lane, factor):
+    tiles = list(tiles)
+    count = len(tiles)
+    for p in range(count):
+        base = first_lane + SUB * p
+        others = range(p + 1, count) if factor else [t for t in range(count) if t != p]
+        own = [lane_splat(tiles[p], base + k) for k in range(SUB)]
+        block = {(i, k): row_splat(own[k], i) for k in range(SUB) for i in range(k, SUB)}
+        rows = [row_splat(tiles[p], i) for i in range(SUB)]
+        scaled = {}
+        diag = []
+        for k in range(SUB):
+            if factor:
+                root = lax.rsqrt(block[k, k])
+                diag.append(root)
+                inverse = root * root
+            else:
+                inverse = 1.0 / block[k, k]
+                diag.append(inverse)
+            for i in range(k + 1, SUB):
+                scaled[i, k] = block[i, k] * inverse
+            for i in range(k + 1, SUB):
+                for q in range(k + 1, i + 1):
+                    block[i, q] = block[i, q] - scaled[i, k] * block[q, k]
+                rows[i] = rows[i] - scaled[i, k] * rows[k]
+        rows = [rows[k] * diag[k] for k in range(SUB)]
+        if factor:
+            finished = assemble(rows)
+            if p + 1 == count:
+                tiles[p] = finished
+                break
+            rows = [rows[k] * diag[k] for k in range(SUB)]
+        for k in range(SUB - 1, 0, -1):
+            for i in range(k):
+                rows[i] = rows[i] - scaled[k, i] * rows[k]
+        for t in others:
+            tile = tiles[t]
+            for k in range(SUB):
+                tile = tile - lane_splat(tiles[t], base + k) * rows[k]
+            tiles[t] = tile
+        tiles[p] = finished if factor else assemble(rows)
+    return jnp.concatenate(tiles, axis=0)
+
+
+def split_tiles(matrix):
+    return [matrix[SUB * t : SUB * (t + 1)] for t in range(matrix.shape[0] // SUB)]
+
+
+def solve_spd(matrix, width):
+    return eliminate(split_tiles(matrix), width, False)[:, :width]
+
+
+def pad_rows(pieces):
+    rows = sum(piece.shape[0] for piece in pieces)
+    if rows < LANES:
+        pieces = pieces + [jnp.zeros((LANES - rows, pieces[0].shape[1]), jnp.float32)]
+    return jnp.concatenate(pieces, axis=0)
+
+
+def local_kernel(
+    sizes, mask_ref, blocks_ref, start_ref, states_ref, ritz_ref, matrix, block, final
+):
+    row_count, col_count, piece, width = sizes
+    local_rows = piece * col_count
+    local_cols = piece * row_count
+    total = piece * row_count * col_count
+    stored = lax.broadcasted_iota(jnp.int32, (piece, local_cols), 1)
+    for q in range(row_count):
+        for c in range(col_count):
+            tile_row = (q * col_count + c) * piece // TILE
+            for d in range(col_count):
+                tile_column = ((stored // piece * col_count + d) * piece + stored % piece) // TILE
+                weights = jnp.zeros((piece, local_cols), jnp.float32)
+                for t in range(total // TILE):
+                    value = mask_ref[tile_row, t].astype(jnp.float32)
+                    weights = jnp.where(tile_column == t, value, weights)
+                first = (q * col_count + d) * local_rows + c * piece
+                matrix[
+                    c * local_cols + q * piece : c * local_cols + (q + 1) * piece,
+                    d * local_cols : (d + 1) * local_cols,
+                ] = blocks_ref[first : first + piece, :] * weights
+            block[c * local_cols + q * piece : c * local_cols + (q + 1) * piece, :] = start_ref[
+                (q * col_count + c) * piece : (q * col_count + c + 1) * piece, :
+            ]
+    states = block[...].T
+    image = dot_nn(states, matrix[...])
+    small = dot_nt(states, pad_rows([image, states]))
+    theta = solve_spd(small, width)
+    resid = image - dot_nn(theta.T, states)
+    along = None
+    for step in range(ITERS):
+        resid_image = dot_nn(resid, matrix[...])
+        if along is None:
+            basis = jnp.concatenate([states, resid], axis=0)
+            basis_image = jnp.concatenate([image, resid_image], axis=0)
+        else:
+            basis = jnp.concatenate([states, resid, along], axis=0)
+            basis_image = jnp.concatenate([image, resid_image, along_image], axis=0)
+        small = dot_nt(basis, pad_rows([states, basis_image + 2.0 * basis]))
+        solved = solve_spd(small, width)
+        both = jnp.concatenate([basis, basis_image], axis=1)
+        tail = dot_nn(solved[width:].T, both[width:])
+        whole = dot_nn(solved.T, both)
+        zeros = jnp.zeros((width, total), jnp.float32)
+        normal = dot_nt(whole[:, :total], pad_rows([zeros, whole[:, :total]]))
+        lane = lax.broadcasted_iota(jnp.int32, (width, LANES), 1)
+        sub = lax.broadcasted_iota(jnp.int32, (width, LANES), 0)
+        normal = jnp.where(lane == sub, 1.0, normal)
+        inverse = eliminate(split_tiles(normal), width, True)[:, :width]
+        whole = dot_nn(inverse, whole)
+        states, image = whole[:, :total], whole[:, total:]
+        ritz = dot_nt(states, image)
+        if step + 1 < ITERS:
+            resid = image - dot_nn(ritz.T, states)
+            tail = dot_nn(inverse, tail)
+            along, along_image = tail[:, :total], tail[:, total:]
+    ritz_ref[...] = 0.5 * (ritz + ritz.T)
+    final[...] = (states * jnp.sqrt(jnp.float32(total))).T
+    mine = lax.axis_index("col") * local_cols + lax.axis_index("row") * piece
+    states_ref[...] = final[pl.ds(pl.multiple_of(mine, SUB), piece), :]
+
+
+def local_body(hamiltonian, tile_mask, start_block):
+    row_count = lax.axis_size("row")
+    col_count = lax.axis_size("col")
+    piece, width = start_block.shape
+    total = piece * row_count * col_count
+    blocks = lax.all_gather(hamiltonian, ("row", "col"), axis=0, tiled=True)
+    start = lax.all_gather(start_block, ("row", "col"), axis=0, tiled=True)
+    vmem = pl.BlockSpec(memory_space=pltpu.VMEM)
+    return pl.pallas_call(
+        functools.partial(local_kernel, (row_count, col_count, piece, width)),
+        out_shape=(
+            jax.ShapeDtypeStruct((piece, width), jnp.float32),
+            jax.ShapeDtypeStruct((width, width), jnp.float32),
+        ),
+        in_specs=[pl.BlockSpec(memory_space=pltpu.SMEM), vmem, vmem],
+        out_specs=(vmem, vmem),
+        scratch_shapes=[
+            pltpu.VMEM((total, total), jnp.float32),
+            pltpu.VMEM((total, width), jnp.float32),
+            pltpu.VMEM((total, width), jnp.float32),
+        ],
+        compiler_params=pltpu.CompilerParams(vmem_limit_bytes=32 * 2**20),
+    )(tile_mask, blocks, start)
 
 
 def small_dot(left, right):
@@ -94,7 +275,16 @@
 
 
 def solution(mesh):
+    row_count, col_count = mesh.shape["row"], mesh.shape["col"]
+
+    def shard(hamiltonian, tile_mask, start_block):
+        piece = start_block.shape[0]
+        size = (piece * row_count * col_count) ** 2 * 4
+        whole = piece % SUB == 0 and piece * row_count % LANES == 0 and TILE % piece == 0
+        run = local_body if whole and size <= LOCAL_BYTES else body
+        return run(hamiltonian, tile_mask, start_block)
+
     placed = (P("row", "col"), P(), P(("row", "col"), None))
     return jax.shard_map(
-        body, mesh=mesh, in_specs=placed, out_specs=(P(("row", "col"), None), P()), check_vma=False
-    )
+        shard, mesh=mesh, in_specs=placed, out_specs=(P(("row", "col"), None), P()), check_vma=False
+    )

time: 556 us -> 115 us (0.21)
  waiting for transfers between devices: 321 us -> 0.68 us
  other arithmetic: 74.3 us -> 0 us
  blocking collectives: 118 us -> 71.8 us
  Pallas kernels: 0 us -> 26.8 us
  matrix products: 19 us -> 0 us
  local copies, waits for them, and re-layouts: 7.59 us -> 1.23 us
    psum x2 -> x0, waiting for transfers between devices: 247 us -> none  [gram_sum(): return lax.psum((first, second), ('row', 'col'))]
    psum x2 -> x0, blocking collectives: 77.7 us -> none  [gram_sum(): return lax.psum((first, second), ('row', 'col'))]
    reduce_scatter x4 -> x0, waiting for transfers between devices: 74.3 us -> none  [operate(): lax.psum_scatter(jnp.dot(masked, gathered, precision=HIGH), 'col', scatte...]
    another operation x35 -> x0, other arithmetic: 73.7 us -> none  [the longest x9 25.4 us: ritz_step(): solved = cho_apply(jnp.linalg.cholesky(shifted), gram[:, :width])]
    all_gather x4 -> x1, blocking collectives: 39.9 us -> 71.8 us  [local_body(): start = lax.all_gather(start_block, ('row', 'col'), axis=0, tiled=True)]
    pallas_call x0 -> x1, Pallas kernels: none -> 26.8 us  [local_body(): pl.pallas_call(functools.partial(local_kernel, (row_count, col_count, pie...]
    dot_general x36 -> x0, matrix products: 16.5 us -> none  [the longest x8 7.37 us: inner(): lax.dot_general(left, right, (((0,), (0,)), ((), ())), precision=HIGH)]
  transfers between devices with their start and end apart: 6 -> 1, of which waited for: 6 -> 0; matrix products, arithmetic and copies ran while one was open for 0% -> 0% of each run, Pallas kernels for 0% -> 0%
where the time goes in v1:
time: 115 us
  blocking collectives  71.8 us (62%)
  Pallas kernels  26.8 us (23%)
  between operations  14.1 us (12%)
  local copies, waits for them, and re-layouts  1.23 us (1%)
    all_gather x1, blocking collectives, local_body(): start = lax.all_gather(start_block, ('row', 'col'), axis=0, tiled=True)  71.8 us
    pallas_call x1, Pallas kernels, local_body(): pl.pallas_call(functools.partial(local_kernel, (row_count, col_count, pie...  26.8 us
  transfers between devices with their start and end apart: 1, of which 0 were waited for; matrix products, arithmetic and copies ran while one was open for 0% of the time, Pallas kernels for 0%

profile of v1, /device:TPU:0, one launch (start us, length us, event | category | flops | bytes accessed | tf_op | source)
XLA Modules:
  0.0 114.6 jit_solution(16469669279198012104)
XLA Ops:
  7.2 0.0 copy-start.2
  7.2 0.0 all-gather.2.cloned.1.call-start
  7.2 0.7 all-gather.2.cloned.1.call-update
  7.9 0.0 copy-done.2
  7.9 0.0 copy-start.1
  7.9 71.8 %all_gather.7.start_ref = f32[512,32]{1,0:T(8,128)S(1)} all-gather(f32[16,32]{1,0:T(8,128)S(1)} %copy-done.2), channel_id=1, replica_groups=mesh['row'=8,'col'=4] {'row','col'}, dimensions={0}, use_global_device_ids=true | all-gather | bytes 67584 | tf_op jit(solution)/shard_map/all_gather | solution.py:175
  79.8 0.0 all-gather.2.cloned.1.call-done.blocks_ref
  79.8 0.0 copy-done.1
  79.8 0.0 copy-start
  79.8 1.2 %copy-done = f32[2048,128]{1,0:T(8,128)S(1)} copy-done((f32[2048,128]{1,0:T(8,128)S(1)}, f32[2048,128]{1,0:T(8,128)}, u32[]{:S(2)}) %copy-start) | copy-done | bytes 1048600
  81.0 26.8 %shard_map.50 = (f32[16,32]{1,0:T(8,128)}, f32[32,32]{1,0:T(8,128)}) custom-call(s32[2,2]{1,0:T(2,128)S(1)} %copy-done.1, f32[2048,128]{1,0:T(8,128)S(1)} %copy-done, f32[512,32]{1,0:T(8,128)S(1)} %all_gather.7.start_ref), custom_call_target="tpu_custom_call" | custom-call | tf_op jit(solution)/shard_map/pallas_call | solution.py:177
Async XLA Ops:
  7.2 0.7 copy-start.2
  7.2 72.6 %all-gather.2.cloned.1.call-start = ((), (), s32[]{:S(2)}) async-start(), calls=%async_computation | async-start | bytes 1081344 | tf_op jit(solution)/shard_map/all_gather | solution.py:174
  7.9 71.8 %copy-start.1 = (s32[2,2]{1,0:T(2,128)S(1)}, s32[2,2]{1,0:T(2,128)}, u32[]{:S(2)}) copy-start(s32[2,2]{1,0:T(2,128)} %mask_ref.1) | copy-start | bytes 52
  79.8 1.2 %copy-start = (f32[2048,128]{1,0:T(8,128)S(1)}, f32[2048,128]{1,0:T(8,128)}, u32[]{:S(2)}) copy-start(f32[2048,128]{1,0:T(8,128)} %all-gather.2.cloned.1.call-done.blocks_ref) | copy-start | bytes 3145732
Sparse Core Ops, SparseCore 0:
  11.0 56.5 all-gather.1

commit v2 on v1

--- a/solution.py
+++ b/solution.py
@@ -14,6 +14,113 @@
 LOCAL_BYTES = 4 * 2**20
 
 HIGH = lax.Precision.HIGHEST
+MESH = pl.DeviceIdType.MESH
+
+
+def flip(index, bit):
+    return index + bit * (1 - 2 * ((index // bit) % 2))
+
+
+def flip_all(index, bits):
+    bit = 1
+    while bit <= bits:
+        if bits & bit:
+            index = flip(index, bit)
+        bit *= 2
+    return index
+
+
+def gather_kernel(
+    row_count, col_count, matrix_ref, start_ref, out_ref, packed, local_sem, send_sem, recv_sem
+):
+    row, col = lax.axis_index("row"), lax.axis_index("col")
+    rows = matrix_ref.shape[0]
+    piece, width = start_ref.shape
+    bits = [1 << i for i in range(row_count.bit_length() - 1)][::-1]
+    orders = [bits, bits[:-1][::-1] + bits[-1:]]
+    packed[0:rows, :] = matrix_ref[...]
+    packed[rows:, :] = jnp.zeros((SUB, LANES), jnp.float32)
+    for part in range(piece // SUB):
+        packed[rows:, part * width : (part + 1) * width] = start_ref[
+            part * SUB : (part + 1) * SUB, :
+        ]
+
+    barrier = pltpu.get_barrier_semaphore()
+    for offset in range(1, col_count):
+        pl.semaphore_signal(
+            barrier, inc=1, device_id=(row, (col + offset) % col_count), device_id_type=MESH
+        )
+    for bit in bits:
+        pl.semaphore_signal(barrier, inc=1, device_id=(flip(row, bit), col), device_id_type=MESH)
+    pl.semaphore_wait(barrier, col_count - 1 + len(bits))
+
+    def place(offset, member):
+        source_col = (col + col_count - offset) % col_count
+        return out_ref.at[flip_all(row, member) * col_count + source_col]
+
+    def own_place():
+        return out_ref.at[row * col_count + col]
+
+    def copy(source, place_there, offset, member, device):
+        return pltpu.make_async_remote_copy(
+            src_ref=source,
+            dst_ref=place_there,
+            send_sem=send_sem.at[offset, member],
+            recv_sem=recv_sem.at[offset, member],
+            device_id=device,
+            device_id_type=MESH,
+        )
+
+    sent = []
+    for offset in range(1, col_count):
+        away = copy(packed, own_place(), offset, 0, (row, (col + offset) % col_count))
+        away.start()
+        sent.append(away)
+    keep = pltpu.make_async_copy(packed, own_place(), local_sem)
+    arrivals = [(offset, member) for member in range(row_count) for offset in range(col_count)]
+
+    def hops(item):
+        offset, member = item
+        return (member % 2, bin(member).count("1") + (offset > 0), offset)
+
+    for offset, member in sorted(arrivals, key=hops):
+        first = offset == 0 and member == 0
+        source = packed if first else place(offset, member)
+        if not first:
+            copy(source, source, offset, member, (row, (col + 1) % col_count)).wait_recv()
+        order = orders[offset % 2]
+        done = [i for i, bit in enumerate(order) if member & bit]
+        for bit in order[(done[-1] + 1 if done else 0) :]:
+            onward = copy(
+                source, place(offset, member), offset, member | bit, (flip(row, bit), col)
+            )
+            onward.start()
+            sent.append(onward)
+        if first:
+            keep.start()
+    for onward in sent:
+        onward.wait_send()
+    keep.wait()
+
+
+def gather_blocks(hamiltonian, start_block):
+    row_count, col_count = lax.axis_size("row"), lax.axis_size("col")
+    vmem = pl.BlockSpec(memory_space=pltpu.VMEM)
+    shape = (hamiltonian.shape[0] + SUB, LANES)
+    sems = pltpu.SemaphoreType.DMA((col_count, row_count))
+    return pl.pallas_call(
+        functools.partial(gather_kernel, row_count, col_count),
+        out_shape=jax.ShapeDtypeStruct((row_count * col_count, *shape), jnp.float32),
+        in_specs=[vmem, vmem],
+        out_specs=pl.BlockSpec(memory_space=pl.ANY),
+        scratch_shapes=[
+            pltpu.VMEM(shape, jnp.float32),
+            pltpu.SemaphoreType.DMA,
+            sems,
+            sems,
+        ],
+        compiler_params=pltpu.CompilerParams(collective_id=0, has_side_effects=True),
+    )(hamiltonian, start_block)
 
 
 def dot_nn(left, right):
@@ -104,7 +211,7 @@
 
 
 def local_kernel(
-    sizes, mask_ref, blocks_ref, start_ref, states_ref, ritz_ref, matrix, block, final
+    sizes, mask_ref, blocks_ref, states_ref, ritz_ref, matrix, block, final
 ):
     row_count, col_count, piece, width = sizes
     local_rows = piece * col_count
@@ -120,14 +227,15 @@
                 for t in range(total // TILE):
                     value = mask_ref[tile_row, t].astype(jnp.float32)
                     weights = jnp.where(tile_column == t, value, weights)
-                first = (q * col_count + d) * local_rows + c * piece
                 matrix[
                     c * local_cols + q * piece : c * local_cols + (q + 1) * piece,
                     d * local_cols : (d + 1) * local_cols,
-                ] = blocks_ref[first : first + piece, :] * weights
-            block[c * local_cols + q * piece : c * local_cols + (q + 1) * piece, :] = start_ref[
-                (q * col_count + c) * piece : (q * col_count + c + 1) * piece, :
-            ]
+                ] = blocks_ref[q * col_count + d, c * piece : (c + 1) * piece, :] * weights
+            for part in range(piece // SUB):
+                first = c * local_cols + q * piece + part * SUB
+                block[first : first + SUB, :] = blocks_ref[
+                    q * col_count + c, local_rows:, part * width : (part + 1) * width
+                ]
     states = block[...].T
     image = dot_nn(states, matrix[...])
     small = dot_nt(states, pad_rows([image, states]))
@@ -171,8 +279,7 @@
     col_count = lax.axis_size("col")
     piece, width = start_block.shape
     total = piece * row_count * col_count
-    blocks = lax.all_gather(hamiltonian, ("row", "col"), axis=0, tiled=True)
-    start = lax.all_gather(start_block, ("row", "col"), axis=0, tiled=True)
+    blocks = gather_blocks(hamiltonian, start_block)
     vmem = pl.BlockSpec(memory_space=pltpu.VMEM)
     return pl.pallas_call(
         functools.partial(local_kernel, (row_count, col_count, piece, width)),
@@ -180,7 +287,7 @@
             jax.ShapeDtypeStruct((piece, width), jnp.float32),
             jax.ShapeDtypeStruct((width, width), jnp.float32),
         ),
-        in_specs=[pl.BlockSpec(memory_space=pltpu.SMEM), vmem, vmem],
+        in_specs=[pl.BlockSpec(memory_space=pltpu.SMEM), vmem],
         out_specs=(vmem, vmem),
         scratch_shapes=[
             pltpu.VMEM((total, total), jnp.float32),
@@ -188,7 +295,7 @@
             pltpu.VMEM((total, width), jnp.float32),
         ],
         compiler_params=pltpu.CompilerParams(vmem_limit_bytes=32 * 2**20),
-    )(tile_mask, blocks, start)
+    )(tile_mask, blocks)
 
 
 def small_dot(left, right):
@@ -280,7 +387,9 @@
     def shard(hamiltonian, tile_mask, start_block):
         piece = start_block.shape[0]
         size = (piece * row_count * col_count) ** 2 * 4
-        whole = piece % SUB == 0 and piece * row_count % LANES == 0 and TILE % piece == 0
+        whole = piece % SUB == 0 and piece * row_count == LANES and TILE % piece == 0
+        whole = whole and start_block.shape[1] * (piece // SUB) <= LANES
+        whole = whole and row_count & (row_count - 1) == 0 and row_count > 1 and col_count > 1
         run = local_body if whole and size <= LOCAL_BYTES else body
         return run(hamiltonian, tile_mask, start_block)
 

time: 115 us -> 48.8 us (0.42)
  blocking collectives: 71.8 us -> 0 us
  Pallas kernels: 26.8 us -> 46.6 us
  between operations: 14.1 us -> 0.66 us
    all_gather x1 -> x0, blocking collectives: 71.8 us -> none  [local_body(): start = lax.all_gather(start_block, ('row', 'col'), axis=0, tiled=True)]
    pallas_call x0 -> x1, Pallas kernels: none -> 19.6 us  [gather_blocks(): pl.pallas_call(functools.partial(gather_kernel, row_count, col_count), ou...]
  transfers between devices with their start and end apart: 1 -> 0, of which waited for: 0 -> 0; matrix products, arithmetic and copies ran while one was open for 0% -> 0% of each run, Pallas kernels for 0% -> 0%
where the time goes in v2:
time: 48.8 us; the launch traced here: 48.5 us
  Pallas kernels  46.6 us (95%)
  local copies, waits for them, and re-layouts  1.27 us (3%)
  between operations  0.66 us (1%)
    pallas_call x1, Pallas kernels, local_body(): pl.pallas_call(functools.partial(local_kernel, (row_count, col_count, pie...  27 us
    pallas_call x1, Pallas kernels, gather_blocks(): pl.pallas_call(functools.partial(gather_kernel, row_count, col_count), ou...  19.6 us
    unnamed x4, local copies, waits for them, and re-layouts  1.27 us

profile of v2, /device:TPU:0, one launch (start us, length us, event | category | flops | bytes accessed | tf_op | source)
XLA Modules:
  0.0 48.5 jit_solution(16456330433960890760)
XLA Ops:
  0.6 0.0 copy-start.1
  0.6 19.6 %shard_map.50.blocks_ref = f32[32,72,128]{2,1,0:T(8,128)} custom-call(f32[64,128]{1,0:T(8,128)} %matrix_ref.1, f32[16,32]{1,0:T(8,128)} %start_ref.1), custom_call_target="tpu_custom_call" | custom-call | tf_op jit(solution)/shard_map/pallas_call | solution.py:111
  20.3 0.0 copy-done.1
  20.3 0.0 copy-start
  20.3 1.3 %copy-done = f32[32,72,128]{2,1,0:T(8,128)S(1)} copy-done((f32[32,72,128]{2,1,0:T(8,128)S(1)}, f32[32,72,128]{2,1,0:T(8,128)}, u32[]{:S(2)}) %copy-start) | copy-done | bytes 1179672
  21.6 27.0 %shard_map.51 = (f32[16,32]{1,0:T(8,128)}, f32[32,32]{1,0:T(8,128)}) custom-call(s32[2,2]{1,0:T(2,128)S(1)} %copy-done.1, f32[32,72,128]{2,1,0:T(8,128)S(1)} %copy-done), custom_call_target="tpu_custom_call" | custom-call | tf_op jit(solution)/shard_map/pallas_call | solution.py:284
Async XLA Ops:
  0.6 19.7 %copy-start.1 = (s32[2,2]{1,0:T(2,128)S(1)}, s32[2,2]{1,0:T(2,128)}, u32[]{:S(2)}) copy-start(s32[2,2]{1,0:T(2,128)} %mask_ref.1) | copy-start | bytes 52
  20.3 1.3 %copy-start = (f32[32,72,128]{2,1,0:T(8,128)S(1)}, f32[32,72,128]{2,1,0:T(8,128)}, u32[]{:S(2)}) copy-start(f32[32,72,128]{2,1,0:T(8,128)} %shard_map.50.blocks_ref) | copy-start | bytes 3538948

commit v3 on v2

--- a/solution.py
+++ b/solution.py
@@ -112,7 +112,7 @@
         functools.partial(gather_kernel, row_count, col_count),
         out_shape=jax.ShapeDtypeStruct((row_count * col_count, *shape), jnp.float32),
         in_specs=[vmem, vmem],
-        out_specs=pl.BlockSpec(memory_space=pl.ANY),
+        out_specs=vmem,
         scratch_shapes=[
             pltpu.VMEM(shape, jnp.float32),
             pltpu.SemaphoreType.DMA,
@@ -253,7 +253,6 @@
         small = dot_nt(basis, pad_rows([states, basis_image + 2.0 * basis]))
         solved = solve_spd(small, width)
         both = jnp.concatenate([basis, basis_image], axis=1)
-        tail = dot_nn(solved[width:].T, both[width:])
         whole = dot_nn(solved.T, both)
         zeros = jnp.zeros((width, total), jnp.float32)
         normal = dot_nt(whole[:, :total], pad_rows([zeros, whole[:, :total]]))
@@ -266,7 +265,7 @@
         ritz = dot_nt(states, image)
         if step + 1 < ITERS:
             resid = image - dot_nn(ritz.T, states)
-            tail = dot_nn(inverse, tail)
+            tail = dot_nn(inverse, dot_nn(solved[width:].T, both[width:]))
             along, along_image = tail[:, :total], tail[:, total:]
     ritz_ref[...] = 0.5 * (ritz + ritz.T)
     final[...] = (states * jnp.sqrt(jnp.float32(total))).T

time: 48.8 us -> 48.3 us (0.990)
  Pallas kernels: 46.6 us -> 46.1 us
    pallas_call x1, Pallas kernels: 27 us -> 26.4 us  [local_body(): pl.pallas_call(functools.partial(local_kernel, (row_count, col_count, pie...]
where the time goes in v3:
time: 48.3 us; the launch traced here: 48.1 us
  Pallas kernels  46.1 us (95%)
  local copies, waits for them, and re-layouts  1.27 us (3%)
  between operations  0.66 us (1%)
    pallas_call x1, Pallas kernels, local_body(): pl.pallas_call(functools.partial(local_kernel, (row_count, col_count, pie...  26.4 us
    pallas_call x1, Pallas kernels, gather_blocks(): pl.pallas_call(functools.partial(gather_kernel, row_count, col_count), ou...  19.7 us
    unnamed x4, local copies, waits for them, and re-layouts  1.27 us

profile of v3, /device:TPU:0, one launch (start us, length us, event | category | flops | bytes accessed | tf_op | source)
XLA Modules:
  0.0 48.1 jit_solution(7736050011817505094)
XLA Ops:
  0.6 0.0 copy-start.1
  0.6 19.7 %shard_map.50.blocks_ref = f32[32,72,128]{2,1,0:T(8,128)} custom-call(f32[64,128]{1,0:T(8,128)} %matrix_ref.1, f32[16,32]{1,0:T(8,128)} %start_ref.1), custom_call_target="tpu_custom_call" | custom-call | tf_op jit(solution)/shard_map/pallas_call | solution.py:111
  20.4 0.0 copy-done.1
  20.4 0.0 copy-start
  20.4 1.3 %copy-done = f32[32,72,128]{2,1,0:T(8,128)S(1)} copy-done((f32[32,72,128]{2,1,0:T(8,128)S(1)}, f32[32,72,128]{2,1,0:T(8,128)}, u32[]{:S(2)}) %copy-start) | copy-done | bytes 1179672
  21.7 26.4 %shard_map.51 = (f32[16,32]{1,0:T(8,128)}, f32[32,32]{1,0:T(8,128)}) custom-call(s32[2,2]{1,0:T(2,128)S(1)} %copy-done.1, f32[32,72,128]{2,1,0:T(8,128)S(1)} %copy-done), custom_call_target="tpu_custom_call" | custom-call | tf_op jit(solution)/shard_map/pallas_call | solution.py:283
Async XLA Ops:
  0.6 19.8 %copy-start.1 = (s32[2,2]{1,0:T(2,128)S(1)}, s32[2,2]{1,0:T(2,128)}, u32[]{:S(2)}) copy-start(s32[2,2]{1,0:T(2,128)} %mask_ref.1) | copy-start | bytes 52
  20.4 1.3 %copy-start = (f32[32,72,128]{2,1,0:T(8,128)S(1)}, f32[32,72,128]{2,1,0:T(8,128)}, u32[]{:S(2)}) copy-start(f32[32,72,128]{2,1,0:T(8,128)} %shard_map.50.blocks_ref) | copy-start | bytes 3538948
